TPU v7x, 32 devices: a whole 2x2x4 slice. The times are simulated.
32 devices in a mesh: ctx: 8 (over z, x), head: 4 (over y, core).
Axes of the slice: x: 2, y: 2, z: 4, core: 2. Of those that a mesh axis runs over, the one named last changes fastest.
Arguments:
- queries: bfloat16 [4096, 64, 128], P(('ctx', 'head')), may hold values from -100 to 100
- keys: bfloat16 [4096, 8, 128], P(('ctx', 'head')), may hold values from -6 to 6
- values: bfloat16 [4096, 8, 128], P(('ctx', 'head')), may hold values from -6 to 6
- outputs: bfloat16 [4096, 64, 128], P(('ctx', 'head')), may hold values from -6 to 6
- out_grad: bfloat16 [4096, 64, 128], P(('ctx', 'head')), may hold values from -6 to 6
- segments: int32 [4096], replicated, may hold values from 0 to 127, never falling along the last dimension, each value on 1 to 128 neighbouring positions
Outputs:
- query_grad: bfloat16 [4096, 64, 128], P(('ctx', 'head'))
- key_grad: bfloat16 [4096, 8, 128], P(('ctx', 'head'))
- value_grad: bfloat16 [4096, 8, 128], P(('ctx', 'head'))
Inputs may be any that keep to these rules, and one draw needn't show every extreme that they name: `segments`: the document number never falls along the pack; every document has 1 to 128 tokens and one has exactly 128.
All inputs are finite; a program needn't handle non-finite values.
Results may differ from a plain program's by a relative error of at most 0.007.
Values may be sent and summed in bfloat16 or wider, within the bound.
A program may use at most 128 MiB of HBM per device.

v0:
```python
import jax
import jax.numpy as jnp
from jax import lax
from jax.sharding import PartitionSpec as P


def shifted(block, axis, distance):
    devices = range(lax.axis_size(axis))
    route = [(i - distance, i) for i in devices if i - distance in devices]
    return lax.ppermute(block, axis, route)


def heads_layout(queries, keys, values, outputs, out_grad, segments):
    head_count = lax.axis_size("head")
    kv_heads = keys.shape[1]
    repeats = max(1, head_count // kv_heads)
    keys_wide = jnp.repeat(keys, repeats, axis=1)
    values_wide = jnp.repeat(values, repeats, axis=1)
    q_local, k_local, v_local, o_local, g_local = (
        lax.all_to_all(queries, "head", split_axis=1, concat_axis=0, tiled=True),
        lax.all_to_all(keys_wide, "head", split_axis=1, concat_axis=0, tiled=True),
        lax.all_to_all(values_wide, "head", split_axis=1, concat_axis=0, tiled=True),
        lax.all_to_all(outputs, "head", split_axis=1, concat_axis=0, tiled=True),
        lax.all_to_all(out_grad, "head", split_axis=1, concat_axis=0, tiled=True),
    )
    seq_rows = q_local.shape[0]
    span = seq_rows // 4
    block = min(512, seq_rows)
    window = span + block
    kv_local = k_local.shape[1]
    group = q_local.shape[1] // kv_local
    head_dim = q_local.shape[2]
    scale = head_dim ** (-0.5)
    prev_keys, prev_values = shifted((k_local, v_local), "ctx", 1)
    prev_keys = prev_keys[seq_rows - span :]
    prev_values = prev_values[seq_rows - span :]
    keys_ext = jnp.concatenate([prev_keys, k_local], axis=0)
    values_ext = jnp.concatenate([prev_values, v_local], axis=0)
    shard_start = lax.axis_index("ctx") * seq_rows
    seg_pad = jnp.concatenate([jnp.full((span,), -1, jnp.int32), segments], axis=0)
    seg_keys = lax.dynamic_slice_in_dim(seg_pad, shard_start, seq_rows + span, 0)
    seg_query = lax.dynamic_slice_in_dim(segments, shard_start, seq_rows, 0)
    col_index = jnp.arange(window, dtype=jnp.int32)
    row_index = jnp.arange(block, dtype=jnp.int32)
    causal = col_index[None, :] <= row_index[:, None] + span
    block_starts = list(range(0, seq_rows, block))

    def scores(begin):
        q_block = q_local[begin : begin + block].reshape(block, kv_local, group, head_dim)
        k_window = keys_ext[begin : begin + window]
        same_doc = (
            seg_query[begin : begin + block][:, None] == seg_keys[begin : begin + window][None, :]
        )
        raw = scale * jnp.einsum(
            "bkgd,wkd->kgbw", q_block, k_window, preferred_element_type=jnp.float32
        )
        return (jnp.where(same_doc & causal, raw, -jnp.inf), q_block, k_window)

    log_sums = []
    for begin in block_starts:
        masked, q_block, k_window = scores(begin)
        top = jnp.max(masked, axis=-1)
        log_sums.append(top + jnp.log(jnp.sum(jnp.exp(masked - top[..., None]), axis=-1)))
    delta_all = jnp.sum(o_local.astype(jnp.float32) * g_local.astype(jnp.float32), axis=-1)
    grad_keys = jnp.zeros((span + seq_rows, kv_local, head_dim), jnp.float32)
    grad_values = jnp.zeros((span + seq_rows, kv_local, head_dim), jnp.float32)
    query_parts = []
    for number, begin in enumerate(block_starts):
        masked, q_block, k_window = scores(begin)
        v_window = values_ext[begin : begin + window]
        prob = jnp.exp(masked - log_sums[number][..., None])
        prob_low = prob.astype(jnp.bfloat16)
        g_block = g_local[begin : begin + block].reshape(block, kv_local, group, head_dim)
        d_block = jnp.transpose(
            delta_all[begin : begin + block].reshape(block, kv_local, group), (1, 2, 0)
        )
        d_prob = jnp.einsum("bkgd,wkd->kgbw", g_block, v_window, preferred_element_type=jnp.float32)
        d_score = (prob * (d_prob - d_block[..., None])).astype(jnp.bfloat16)
        query_part = scale * jnp.einsum(
            "kgbw,wkd->bkgd", d_score, k_window, preferred_element_type=jnp.float32
        )
        query_parts.append(
            query_part.astype(jnp.bfloat16).reshape(block, kv_local * group, head_dim)
        )
        key_part = scale * jnp.einsum(
            "kgbw,bkgd->wkd", d_score, q_block, preferred_element_type=jnp.float32
        )
        value_part = jnp.einsum(
            "kgbw,bkgd->wkd", prob_low, g_block, preferred_element_type=jnp.float32
        )
        grad_keys = grad_keys.at[begin : begin + window].add(key_part)
        grad_values = grad_values.at[begin : begin + window].add(value_part)
    query_local = jnp.concatenate(query_parts, axis=0)
    padding = jnp.zeros((seq_rows - span, kv_local, head_dim), jnp.float32)
    lead_keys = jnp.concatenate([padding, grad_keys[:span]], axis=0)
    lead_values = jnp.concatenate([padding, grad_values[:span]], axis=0)
    back_keys, back_values = (
        shifted(lead_keys.astype(jnp.bfloat16), "ctx", -1).astype(lead_keys.dtype),
        shifted(lead_values.astype(jnp.bfloat16), "ctx", -1).astype(lead_values.dtype),
    )
    own_keys = grad_keys[span:] + back_keys
    own_values = grad_values[span:] + back_values
    query_home = lax.all_to_all(query_local, "head", split_axis=0, concat_axis=1, tiled=True)
    keys_home, values_home = (
        lax.all_to_all(own_keys, "head", split_axis=0, concat_axis=1, tiled=True),
        lax.all_to_all(own_values, "head", split_axis=0, concat_axis=1, tiled=True),
    )
    token_rows = keys_home.shape[0]
    key_grad = jnp.sum(keys_home.reshape(token_rows, kv_heads, repeats, head_dim), axis=2).astype(
        jnp.bfloat16
    )
    value_grad = jnp.sum(
        values_home.reshape(token_rows, kv_heads, repeats, head_dim), axis=2
    ).astype(jnp.bfloat16)
    return (query_home, key_grad, value_grad)


def shards(queries, keys, values, outputs, out_grad, segments):
    return heads_layout(queries, keys, values, outputs, out_grad, segments)


def solution(mesh):
    return jax.shard_map(
        shards,
        mesh=mesh,
        in_specs=(
            P(("ctx", "head"), None, None),
            P(("ctx", "head"), None, None),
            P(("ctx", "head"), None, None),
            P(("ctx", "head"), None, None),
            P(("ctx", "head"), None, None),
            P(),
        ),
        out_specs=(
            P(("ctx", "head"), None, None),
            P(("ctx", "head"), None, None),
            P(("ctx", "head"), None, None),
        ),
        check_vma=False,
    )
```

profile of v0, /device:TPU:15, one launch (start us, length us, event | category | flops | bytes accessed | tf_op | source)
XLA Modules:
  0.0 195.9 jit_solution(7293912819018643855)
XLA Ops:
  0.6 1.7 copy.19
  2.3 4.2 %all-to-all-start = ((bf16[128,8,128]{2,0,1:T(8,128)(2,1)}), bf16[128,8,128]{2,0,1:T(8,128)(2,1)S(1)}, u32[]{:S(2)}, u32[]{:S(2)}) async-start(bf16[128,8,128]{2,0,1:T(8,128)(2,1)} %copy.19), calls=%async_computation | async-start | bytes 524288 | tf_op jit(solution)/shard_map/all_to_all | solution.py:21
  6.5 1.7 copy.23
  8.2 2.4 %all-to-all-done = bf16[128,8,128]{2,0,1:T(8,128)(2,1)S(1)} async-done(((bf16[128,8,128]{2,0,1:T(8,128)(2,1)}), bf16[128,8,128]{2,0,1:T(8,128)(2,1)S(1)}, u32[]{:S(2)}, u32[]{:S(2)}) %all-to-all-start) | async-done | bytes 262176 | tf_op jit(solution)/shard_map/all_to_all | solution.py:21
  10.6 5.3 %all-to-all-start.2 = ((bf16[128,8,128]{2,0,1:T(8,128)(2,1)}), bf16[128,8,128]{2,0,1:T(8,128)(2,1)S(1)}, u32[]{:S(2)}, u32[]{:S(2)}) async-start(bf16[128,8,128]{2,0,1:T(8,128)(2,1)} %copy.23), calls=%async_computation.2 | async-start | bytes 524288 | tf_op jit(solution)/shard_map/all_to_all | solution.py:22
  15.9 4.3 %copy.21 = bf16[128,64,128]{2,0,1:T(8,128)(2,1)} copy(bf16[128,64,128]{2,1,0:T(8,128)(2,1)} %param.14) | data formatting | bytes 4194304 | tf_op args[0]
  20.2 0.0 all-to-all-done.2
  20.2 5.4 %all-to-all-start.1 = ((bf16[128,64,128]{2,0,1:T(8,128)(2,1)}), bf16[128,64,128]{2,0,1:T(8,128)(2,1)S(1)}, u32[]{:S(2)}, u32[]{:S(2)}) async-start(bf16[128,64,128]{2,0,1:T(8,128)(2,1)} %copy.21), calls=%async_computation.1 | async-start | bytes 4194304 | tf_op jit(solution)/shard_map/all_to_all | solution.py:20
  25.6 4.3 %copy.25 = bf16[128,64,128]{2,0,1:T(8,128)(2,1)} copy(bf16[128,64,128]{2,1,0:T(8,128)(2,1)} %param.18) | data formatting | bytes 4194304 | tf_op args[4]
  29.9 19.5 %all-to-all-done.1 = bf16[128,64,128]{2,0,1:T(8,128)(2,1)S(1)} async-done(((bf16[128,64,128]{2,0,1:T(8,128)(2,1)}), bf16[128,64,128]{2,0,1:T(8,128)(2,1)S(1)}, u32[]{:S(2)}, u32[]{:S(2)}) %all-to-all-start.1) | async-done | bytes 2097184 | tf_op jit(solution)/shard_map/all_to_all | solution.py:20
  49.3 1.3 copy-done.2
  50.7 5.5 %all-to-all-start.3 = ((bf16[128,64,128]{2,0,1:T(8,128)(2,1)}), bf16[128,64,128]{2,0,1:T(8,128)(2,1)S(1)}, u32[]{:S(2)}, u32[]{:S(2)}) async-start(bf16[128,64,128]{2,0,1:T(8,128)(2,1)} %copy.25), calls=%async_computation.3 | async-start | bytes 4194304 | tf_op jit(solution)/shard_map/all_to_all | solution.py:24
  56.2 0.0 copy-done.6
  56.2 0.1 pad_dynamic-slice_fusion
  56.3 3.2 %collective-permute-start = (bf16[512,2,128]{2,0,1:T(8,128)(2,1)S(1)}, bf16[512,2,128]{2,0,1:T(8,128)(2,1)S(1)}, u32[]{:S(2)}, u32[]{:S(2)}) collective-permute-start(bf16[512,2,128]{2,0,1:T(8,128)(2,1)S(1)} %bitcast.104), channel_id=1, source_target_pairs={{0,4},{4,8},{8,12},{12,16},{16,20},{20,24},{24,28},{1,5},{5,9},{9,... | collective-permute-start | bytes 786440 | tf_op jit(solution)/shard_map/ppermute | solution.py:10
  59.5 3.1 %collective-permute-start.1 = (bf16[512,2,128]{2,0,1:T(8,128)(2,1)S(1)}, bf16[512,2,128]{2,0,1:T(8,128)(2,1)S(1)}, u32[]{:S(2)}, u32[]{:S(2)}) collective-permute-start(bf16[512,2,128]{2,0,1:T(8,128)(2,1)S(1)} %bitcast.114), channel_id=1, source_target_pairs={{0,4},{4,8},{8,12},{12,16},{16,20},{20,24},{24,28},{1,5},{5,9},{9,... | collective-permute-start | bytes 786440 | tf_op jit(solution)/shard_map/ppermute | solution.py:10
  62.6 0.0 copy-start.3
  62.6 0.1 dynamic_slice.6
  62.7 4.4 %copy.27 = bf16[128,64,128]{2,0,1:T(8,128)(2,1)} copy(bf16[128,64,128]{2,1,0:T(8,128)(2,1)} %param.17) | data formatting | bytes 4194304 | tf_op args[3]
  67.1 0.3 fusion.8
  67.4 0.0 collective-permute-done
  67.5 3.8 %collective-permute-done.1 = bf16[512,2,128]{2,0,1:T(8,128)(2,1)S(1)} collective-permute-done((bf16[512,2,128]{2,0,1:T(8,128)(2,1)S(1)}, bf16[512,2,128]{2,0,1:T(8,128)(2,1)S(1)}, u32[]{:S(2)}, u32[]{:S(2)}) %collective-permute-start.1) | collective-permute-done | bytes 262176 | tf_op jit(solution)/shard_map/ppermute | solution.py:10
  71.3 0.6 slice.67
  71.9 0.0 copy-done.3
  71.9 0.1 copy.22
  72.1 0.0 copy-start
  72.1 1.3 copy-done
  73.4 8.8 %fusion.3 = (f32[2,8,512]{2,1,0:T(8,128)S(1)}, f32[2,640,512,8]{2,1,3,0:T(8,128)}) fusion(pred[512,640]{0,1:T(8,128)(4,1)S(1)} %fusion.8, bf16[512,2,8,128]{3,0,2,1:T(8,128)(2,1)S(1)} %bitcast.99, bf16[512,2,128]{2,0,1:T(8,128)(2,1)S(1)} %bitcast.105, bf16[128,2,128]{2,0,1:T(8,128)(2,1)S(1)} %slice.66), kind=kOutput, calls=%fused_computation.7 | convolution fusion | flops 1358553088 | bytes 23756800 | tf_op jit(solution)/shard_map/bkgd,wkd->kgbw/dot_general | solution.py:54
  82.2 0.0 all-to-all-done.3
  82.2 5.6 %all-to-all-start.4 = ((bf16[128,64,128]{2,0,1:T(8,128)(2,1)}), bf16[128,64,128]{2,0,1:T(8,128)(2,1)}, u32[]{:S(2)}, u32[]{:S(2)}) async-start(bf16[128,64,128]{2,0,1:T(8,128)(2,1)} %copy.27), calls=%async_computation.4 | async-start | bytes 4194304 | tf_op jit(solution)/shard_map/all_to_all | solution.py:23
  87.8 9.5 %exponential_reduce_fusion = f32[2,8,512]{2,1,0:T(8,128)S(1)} fusion(f32[2,640,512,8]{2,1,3,0:T(8,128)} %get-tuple-element.44, f32[2,8,512]{2,1,0:T(8,128)S(1)} %get-tuple-element.43, pred[512,640]{0,1:T(8,128)(4,1)S(1)} %fusion.8), kind=kLoop, calls=%fused_computation.5 | loop fusion | flops 20963328 | bytes 21364736 | tf_op jit(solution)/shard_map/reduce_sum | solution.py:63
  97.3 1.5 copy.26
  98.8 0.0 copy-start.5
  98.8 12.7 %fusion.9 = f32[640,2,128]{2,0,1:T(8,128)} fusion(bf16[512,2,8,128]{3,0,2,1:T(8,128)(2,1)} %bitcast.107, f32[2,640,512,8]{2,1,3,0:T(8,128)} %get-tuple-element.44, f32[2,8,512]{2,1,0:T(8,128)S(1)} %log_add_fusion, pred[512,640]{0,1:T(8,128)(4,1)S(1)} %fusion.8), kind=kOutput, calls=%fused_computation.15 | convolution fusion | flops 1363148800 | bytes 24084480 | tf_op jit(solution)/shard_map/kgbw,bkgd->wkd/dot_general | solution.py:88
  111.5 0.0 copy-done.5
  111.5 0.9 slice.76
  112.4 3.0 %collective-permute-start.3 = (bf16[512,2,128]{2,0,1:T(8,128)(2,1)S(1)}, bf16[512,2,128]{2,0,1:T(8,128)(2,1)S(1)}, u32[]{:S(2)}, u32[]{:S(2)}) collective-permute-start(bf16[512,2,128]{2,0,1:T(8,128)(2,1)S(1)} %concatenate.23), channel_id=1, source_target_pairs={{4,0},{8,4},{12,8},{16,12},{20,16},{24,20},{28,24},{5,1},{9,5},{13... | collective-permute-start | bytes 786440 | tf_op jit(solution)/shard_map/ppermute | solution.py:10
  115.5 0.0 all-to-all-done.4
  115.5 2.1 %bitcast_convert_fusion = f32[128,4,16,128]{3,0,2,1:T(8,128)S(1)} fusion(bf16[128,64,128]{2,0,1:T(8,128)(2,1)} %all-to-all-done.4), kind=kLoop, calls=%fused_computation.34 | loop fusion | flops 1048576 | bytes 6291456 | tf_op jit(solution)/shard_map/convert_element_type | solution.py:64
  117.6 1.9 fusion.7
  119.5 0.8 reshape.120
  120.3 0.0 copy-start.1
  120.3 13.3 %fusion.1 = bf16[2,8,512,640]{2,3,1,0:T(8,128)(2,1)} fusion(f32[2,640,512,8]{2,1,3,0:T(8,128)} %get-tuple-element.44, f32[2,8,512]{2,1,0:T(8,128)S(1)} %bitcast.118, f32[2,8,512]{2,1,0:T(8,128)} %copy-done.5, pred[512,640]{0,1:T(8,128)(4,1)S(1)} %fusion.8, bf16[512,2,8,128]{3,0,2,1:T(8,128)(2,1)} %bitcast.108, bf16[512,2,128]{2,0,1:T(8,128)(2,1)S(1)} %bitcast.115, ...), kind=kOutput, calls=%fused_computation.2 | convolution fusion | flops 1374289920 | bytes 34275328 | tf_op jit(solution)/shard_map/bkgd,wkd->kgbw/dot_general | solution.py:77
  133.6 0.0 copy-done.1
  133.6 6.9 %fusion.13 = f32[640,2,128]{2,0,1:T(8,128)S(1)} fusion(bf16[2,8,512,640]{2,3,1,0:T(8,128)(2,1)} %fusion.1, bf16[512,2,8,128]{3,0,2,1:T(8,128)(2,1)S(1)} %bitcast.100), kind=kOutput, calls=%fused_computation.18 | convolution fusion | flops 1342341120 | bytes 13238272 | tf_op jit(solution)/shard_map/kgbw,bkgd->wkd/dot_general | solution.py:85
  140.5 2.3 %collective-permute-start.2 = (bf16[512,2,128]{2,0,1:T(8,128)(2,1)S(1)}, bf16[512,2,128]{2,0,1:T(8,128)(2,1)S(1)}, u32[]{:S(2)}, u32[]{:S(2)}) collective-permute-start(bf16[512,2,128]{2,0,1:T(8,128)(2,1)S(1)} %concatenate.22), channel_id=1, source_target_pairs={{4,0},{8,4},{12,8},{16,12},{20,16},{24,20},{28,24},{5,1},{9,5},{13... | collective-permute-start | bytes 786440 | tf_op jit(solution)/shard_map/ppermute | solution.py:10
  142.9 0.0 collective-permute-done.3
  142.9 0.0 copy-done.4
  142.9 0.1 slice_add_fusion
  143.0 1.0 copy.35
  144.0 4.2 %all-to-all-start.7 = ((bf16[512,2,128]{2,1,0:T(2,128)(2,1)}), bf16[512,2,128]{2,1,0:T(2,128)(2,1)S(1)}, u32[]{:S(2)}, u32[]{:S(2)}) async-start(bf16[512,2,128]{2,1,0:T(2,128)(2,1)} %copy.35), calls=%async_computation.7 | async-start | bytes 524288 | tf_op jit(solution)/shard_map/all_to_all | solution.py:106
  148.2 2.4 %collective-permute-done.2 = bf16[512,2,128]{2,0,1:T(8,128)(2,1)S(1)} collective-permute-done((bf16[512,2,128]{2,0,1:T(8,128)(2,1)S(1)}, bf16[512,2,128]{2,0,1:T(8,128)(2,1)S(1)}, u32[]{:S(2)}, u32[]{:S(2)}) %collective-permute-start.2) | collective-permute-done | bytes 262176 | tf_op jit(solution)/shard_map/ppermute | solution.py:10
  150.5 0.1 slice_add_fusion.1
  150.6 1.0 copy.33
  151.6 0.7 all-to-all-done.7
  152.3 5.3 %all-to-all-start.6 = ((bf16[512,2,128]{2,1,0:T(2,128)(2,1)}), bf16[512,2,128]{2,1,0:T(2,128)(2,1)S(1)}, u32[]{:S(2)}, u32[]{:S(2)}) async-start(bf16[512,2,128]{2,1,0:T(2,128)(2,1)} %copy.33), calls=%async_computation.6 | async-start | bytes 524288 | tf_op jit(solution)/shard_map/all_to_all | solution.py:105
  157.6 5.8 %multiply_convert_fusion = bf16[2,128,8,512]{3,1,2,0:T(8,128)(2,1)S(1)} fusion(bf16[2,8,512,640]{2,3,1,0:T(8,128)(2,1)} %fusion.1, bf16[512,2,128]{2,0,1:T(8,128)(2,1)S(1)} %bitcast.106, bf16[128,2,128]{2,0,1:T(8,128)(2,1)S(1)} %slice.66), kind=kOutput, calls=%fused_computation.12 | convolution fusion | flops 1344929792 | bytes 12910592 | tf_op jit(solution)/shard_map/kgbw,wkd->bkgd/dot_general | solution.py:79
  163.4 3.1 %copy.31 = bf16[512,16,128]{2,1,0:T(8,128)(2,1)} copy(bf16[512,16,128]{0,2,1:T(8,128)(2,1)S(1)} %bitcast.101) | data formatting | bytes 4194304 | tf_op jit(solution)/shard_map/reshape | solution.py:83
  166.5 0.0 all-to-all-done.6
  166.5 3.6 %all-to-all-start.5 = ((bf16[512,16,128]{2,1,0:T(8,128)(2,1)}), bf16[512,16,128]{2,1,0:T(8,128)(2,1)S(1)}, u32[]{:S(2)}, u32[]{:S(2)}) async-start(bf16[512,16,128]{2,1,0:T(8,128)(2,1)} %copy.31), calls=%async_computation.5 | async-start | bytes 4194304 | tf_op jit(solution)/shard_map/all_to_all | solution.py:103
  170.1 0.9 copy.36
  171.0 0.9 copy.34
  171.9 22.0 %all-to-all-done.5 = bf16[512,16,128]{2,1,0:T(8,128)(2,1)S(1)} async-done(((bf16[512,16,128]{2,1,0:T(8,128)(2,1)}), bf16[512,16,128]{2,1,0:T(8,128)(2,1)S(1)}, u32[]{:S(2)}, u32[]{:S(2)}) %all-to-all-start.5) | async-done | bytes 2097184 | tf_op jit(solution)/shard_map/all_to_all | solution.py:103
  193.9 2.0 %copy.32 = bf16[128,4,16,128]{3,2,1,0:T(8,128)(2,1)} copy(bf16[128,4,16,128]{3,2,0,1:T(8,128)(2,1)S(1)} %bitcast.103) | data formatting | bytes 4194304 | tf_op jit(solution)/shard_map/all_to_all | solution.py:103
  (11 shorter events, 0.1 us)
Async XLA Ops:
  2.3 8.3 %all-to-all-start = ((bf16[128,8,128]{2,0,1:T(8,128)(2,1)}), bf16[128,8,128]{2,0,1:T(8,128)(2,1)S(1)}, u32[]{:S(2)}, u32[]{:S(2)}) async-start(bf16[128,8,128]{2,0,1:T(8,128)(2,1)} %copy.19), calls=%async_computation | async-start | bytes 524288 | tf_op jit(solution)/shard_map/all_to_all | solution.py:21
  10.6 9.6 %all-to-all-start.2 = ((bf16[128,8,128]{2,0,1:T(8,128)(2,1)}), bf16[128,8,128]{2,0,1:T(8,128)(2,1)S(1)}, u32[]{:S(2)}, u32[]{:S(2)}) async-start(bf16[128,8,128]{2,0,1:T(8,128)(2,1)} %copy.23), calls=%async_computation.2 | async-start | bytes 524288 | tf_op jit(solution)/shard_map/all_to_all | solution.py:22
  20.2 29.1 %all-to-all-start.1 = ((bf16[128,64,128]{2,0,1:T(8,128)(2,1)}), bf16[128,64,128]{2,0,1:T(8,128)(2,1)S(1)}, u32[]{:S(2)}, u32[]{:S(2)}) async-start(bf16[128,64,128]{2,0,1:T(8,128)(2,1)} %copy.21), calls=%async_computation.1 | async-start | bytes 4194304 | tf_op jit(solution)/shard_map/all_to_all | solution.py:20
  25.6 30.6 %copy-start.6 = (s32[4096]{0:T(1024)S(1)}, s32[4096]{0:T(1024)}, u32[]{:S(2)}) copy-start(s32[4096]{0:T(1024)} %param.19) | copy-start | bytes 49156
  49.3 1.3 copy-start.2
  50.7 31.5 %all-to-all-start.3 = ((bf16[128,64,128]{2,0,1:T(8,128)(2,1)}), bf16[128,64,128]{2,0,1:T(8,128)(2,1)S(1)}, u32[]{:S(2)}, u32[]{:S(2)}) async-start(bf16[128,64,128]{2,0,1:T(8,128)(2,1)} %copy.25), calls=%async_computation.3 | async-start | bytes 4194304 | tf_op jit(solution)/shard_map/all_to_all | solution.py:24
  56.3 11.2 %collective-permute-start = (bf16[512,2,128]{2,0,1:T(8,128)(2,1)S(1)}, bf16[512,2,128]{2,0,1:T(8,128)(2,1)S(1)}, u32[]{:S(2)}, u32[]{:S(2)}) collective-permute-start(bf16[512,2,128]{2,0,1:T(8,128)(2,1)S(1)} %bitcast.104), channel_id=1, source_target_pairs={{0,4},{4,8},{8,12},{12,16},{16,20},{20,24},{24,28},{1,5},{5,9},{9,... | collective-permute-start | bytes 786440 | tf_op jit(solution)/shard_map/ppermute | solution.py:10
  59.5 11.8 %collective-permute-start.1 = (bf16[512,2,128]{2,0,1:T(8,128)(2,1)S(1)}, bf16[512,2,128]{2,0,1:T(8,128)(2,1)S(1)}, u32[]{:S(2)}, u32[]{:S(2)}) collective-permute-start(bf16[512,2,128]{2,0,1:T(8,128)(2,1)S(1)} %bitcast.114), channel_id=1, source_target_pairs={{0,4},{4,8},{8,12},{12,16},{16,20},{20,24},{24,28},{1,5},{5,9},{9,... | collective-permute-start | bytes 786440 | tf_op jit(solution)/shard_map/ppermute | solution.py:10
  62.6 9.3 %copy-start.3 = (bf16[128,64,128]{2,0,1:T(8,128)(2,1)S(1)}, bf16[128,64,128]{2,0,1:T(8,128)(2,1)}, u32[]{:S(2)}) copy-start(bf16[128,64,128]{2,0,1:T(8,128)(2,1)} %copy-done.2) | copy-start | bytes 6291460
  72.1 1.3 copy-start
  82.2 33.3 %all-to-all-start.4 = ((bf16[128,64,128]{2,0,1:T(8,128)(2,1)}), bf16[128,64,128]{2,0,1:T(8,128)(2,1)}, u32[]{:S(2)}, u32[]{:S(2)}) async-start(bf16[128,64,128]{2,0,1:T(8,128)(2,1)} %copy.27), calls=%async_computation.4 | async-start | bytes 4194304 | tf_op jit(solution)/shard_map/all_to_all | solution.py:23
  98.8 12.7 %copy-start.5 = (f32[2,8,512]{2,1,0:T(8,128)}, f32[2,8,512]{2,1,0:T(8,128)S(1)}, u32[]{:S(2)}) copy-start(f32[2,8,512]{2,1,0:T(8,128)S(1)} %log_add_fusion) | copy-start | bytes 98308
  112.4 30.5 %collective-permute-start.3 = (bf16[512,2,128]{2,0,1:T(8,128)(2,1)S(1)}, bf16[512,2,128]{2,0,1:T(8,128)(2,1)S(1)}, u32[]{:S(2)}, u32[]{:S(2)}) collective-permute-start(bf16[512,2,128]{2,0,1:T(8,128)(2,1)S(1)} %concatenate.23), channel_id=1, source_target_pairs={{4,0},{8,4},{12,8},{16,12},{20,16},{24,20},{28,24},{5,1},{9,5},{13... | collective-permute-start | bytes 786440 | tf_op jit(solution)/shard_map/ppermute | solution.py:10
  120.3 13.3 %copy-start.1 = (bf16[128,4,16,128]{3,0,1,2:T(8,128)(2,1)S(1)}, bf16[128,4,16,128]{3,0,1,2:T(8,128)(2,1)}, u32[]{:S(2)}) copy-start(bf16[128,4,16,128]{3,0,1,2:T(8,128)(2,1)} %copy-done) | copy-start | bytes 6291460
  133.6 9.3 %copy-start.4 = (f32[640,2,128]{2,0,1:T(8,128)S(1)}, f32[640,2,128]{2,0,1:T(8,128)}, u32[]{:S(2)}) copy-start(f32[640,2,128]{2,0,1:T(8,128)} %fusion.9) | copy-start | bytes 1966084
  140.5 10.0 %collective-permute-start.2 = (bf16[512,2,128]{2,0,1:T(8,128)(2,1)S(1)}, bf16[512,2,128]{2,0,1:T(8,128)(2,1)S(1)}, u32[]{:S(2)}, u32[]{:S(2)}) collective-permute-start(bf16[512,2,128]{2,0,1:T(8,128)(2,1)S(1)} %concatenate.22), channel_id=1, source_target_pairs={{4,0},{8,4},{12,8},{16,12},{20,16},{24,20},{28,24},{5,1},{9,5},{13... | collective-permute-start | bytes 786440 | tf_op jit(solution)/shard_map/ppermute | solution.py:10
  144.0 8.3 %all-to-all-start.7 = ((bf16[512,2,128]{2,1,0:T(2,128)(2,1)}), bf16[512,2,128]{2,1,0:T(2,128)(2,1)S(1)}, u32[]{:S(2)}, u32[]{:S(2)}) async-start(bf16[512,2,128]{2,1,0:T(2,128)(2,1)} %copy.35), calls=%async_computation.7 | async-start | bytes 524288 | tf_op jit(solution)/shard_map/all_to_all | solution.py:106
  152.3 14.2 %all-to-all-start.6 = ((bf16[512,2,128]{2,1,0:T(2,128)(2,1)}), bf16[512,2,128]{2,1,0:T(2,128)(2,1)S(1)}, u32[]{:S(2)}, u32[]{:S(2)}) async-start(bf16[512,2,128]{2,1,0:T(2,128)(2,1)} %copy.33), calls=%async_computation.6 | async-start | bytes 524288 | tf_op jit(solution)/shard_map/all_to_all | solution.py:105
  166.5 27.4 %all-to-all-start.5 = ((bf16[512,16,128]{2,1,0:T(8,128)(2,1)}), bf16[512,16,128]{2,1,0:T(8,128)(2,1)S(1)}, u32[]{:S(2)}, u32[]{:S(2)}) async-start(bf16[512,16,128]{2,1,0:T(8,128)(2,1)} %copy.31), calls=%async_computation.5 | async-start | bytes 4194304 | tf_op jit(solution)/shard_map/all_to_all | solution.py:103
where the time goes:
time: 199 us; the launch traced here: 196 us
  waiting for transfers between devices  50.9 us (26%)
  starting transfers between devices  50.7 us (25%)
  matrix products  47.5 us (24%)
  local copies, waits for them, and re-layouts  32 us (16%)
  other arithmetic  13.9 us (7%)
    all_to_all x1, waiting for transfers between devices, heads_layout(): lax.all_to_all(query_local, 'head', split_axis=0, concat_axis=1, tiled=True)  22 us
    all_to_all x1, waiting for transfers between devices, heads_layout(): lax.all_to_all(queries, 'head', split_axis=1, concat_axis=0, tiled=True)  19.5 us
    unnamed x19, local copies, waits for them, and re-layouts  19 us
    dot_general x1, matrix products, heads_layout(): jnp.einsum('bkgd,wkd->kgbw', g_block, v_window, preferred_element_type=jn...  13.3 us
    dot_general x1, matrix products, heads_layout(): jnp.einsum('kgbw,bkgd->wkd', prob_low, g_block, preferred_element_type=jn...  12.7 us
    ppermute x4, starting transfers between devices, shifted(): return lax.ppermute(block, axis, route)  11.7 us
    reduce_sum x1, other arithmetic, heads_layout(): jnp.sum(jnp.exp(masked - top[..., None]), axis=-1)  9.52 us
    dot_general x1, matrix products, scores(): jnp.einsum('bkgd,wkd->kgbw', q_block, k_window, preferred_element_type=jn...  8.77 us
  transfers between devices with their start and end apart: 12, of which 6 were waited for; matrix products, arithmetic and copies ran while one was open for 44% of the time, Pallas kernels for 0%

commit v1 on v0

v1 whole, which is shorter than its diff:
```python
import functools
import math

import jax
import jax.numpy as jnp
from jax import lax
from jax.experimental import pallas as pl
from jax.experimental.pallas import tpu as pltpu
from jax.sharding import PartitionSpec as P

SUB = 32
MASKED = -1e30
MESH = pl.DeviceIdType.MESH


def nt(a, b):
    return lax.dot_general(a, b, (((1,), (1,)), ((), ())), preferred_element_type=jnp.float32)


def nn(a, b):
    return jnp.dot(a, b, preferred_element_type=jnp.float32)


def tn(a, b):
    return lax.dot_general(a, b, (((0,), (0,)), ((), ())), preferred_element_type=jnp.float32)


def kernel(
    sizes,
    q_hbm, k_ref, v_ref, o_hbm, g_hbm, seg_ref,
    dq_hbm, dk_ref, dv_ref,
    q_buf, g_buf, o_buf, dq_buf, flat, kv_own, kv_prev, back_out, back_in, own_sum, bias,
    in_sem, dq_sem, fwd_send, fwd_recv, bwd_send, bwd_recv,
):
    ctx_count, head_count, halo, rows, kv_heads, group, dim = sizes
    devices = ctx_count * head_count
    span = halo * rows
    pairs = kv_heads // 2
    wide = 2 * group
    lanes = SUB * group
    width = span + SUB
    parts = rows // SUB
    scale = dim ** (-0.5)
    me = lax.axis_index("ctx") * head_count + lax.axis_index("head")

    def device(i):
        return (i // head_count, i % head_count)

    def load(number, hbm, buf, jj):
        return pltpu.make_async_copy(
            hbm.at[:, pl.ds(jj * wide, wide), :], buf.at[jj], in_sem.at[number, jj]
        )

    def store(jj):
        return pltpu.make_async_copy(
            dq_buf.at[jj], dq_hbm.at[:, pl.ds(jj * wide, wide), :], dq_sem.at[jj]
        )

    def forward(h, jj):
        return pltpu.make_async_remote_copy(
            src_ref=kv_own.at[jj], dst_ref=kv_prev.at[h - 1, jj],
            send_sem=fwd_send.at[h - 1, jj], recv_sem=fwd_recv.at[h - 1, jj],
            device_id=device(me + h), device_id_type=MESH,
        )

    def backward(h, jj):
        return pltpu.make_async_remote_copy(
            src_ref=back_out.at[h - 1, jj], dst_ref=back_in.at[h - 1, jj],
            send_sem=bwd_send.at[h - 1, jj], recv_sem=bwd_recv.at[h - 1, jj],
            device_id=device(me - h), device_id_type=MESH,
        )

    barrier = pltpu.get_barrier_semaphore()
    for h in range(1, halo + 1):
        @pl.when(me >= h)
        def _():
            pl.semaphore_signal(barrier, inc=1, device_id=device(me - h), device_id_type=MESH)

        @pl.when(me + h < devices)
        def _():
            pl.semaphore_signal(barrier, inc=1, device_id=device(me + h), device_id_type=MESH)

    for jj in range(pairs):
        load(0, q_hbm, q_buf, jj).start()
        load(1, g_hbm, g_buf, jj).start()
        load(2, o_hbm, o_buf, jj).start()

    flat[0] = k_ref[...].astype(jnp.float32).reshape(rows * kv_heads, dim)
    flat[1] = v_ref[...].astype(jnp.float32).reshape(rows * kv_heads, dim)

    def split(jj):
        for c in range(2):
            for which in range(2):
                kv_own[jj, 2 * c + which] = flat[
                    which, pl.ds(2 * jj + c, rows, stride=kv_heads), :
                ].astype(jnp.bfloat16)

    split(0)
    pl.semaphore_wait(barrier, jnp.minimum(me, halo) + jnp.minimum(devices - 1 - me, halo))

    for jj in range(pairs):
        if jj:
            split(jj)
        for h in range(1, halo + 1):
            @pl.when(me + h < devices)
            def _():
                forward(h, jj).start()

    for h in range(1, halo + 1):
        @pl.when(me < h)
        def _():
            kv_prev[h - 1] = jnp.zeros(kv_prev.shape[1:], kv_prev.dtype)

    token = lax.broadcasted_iota(jnp.int32, (rows, rows * group), 0)
    lane = lax.broadcasted_iota(jnp.int32, (rows, rows * group), 1)
    spread = jnp.where(lane // group == token, 1.0, 0.0).astype(jnp.bfloat16)
    own_seg = seg_ref[pl.ds(me, 1), :].astype(jnp.float32)
    seg_query = nn(jnp.broadcast_to(own_seg, (8, rows)).astype(jnp.bfloat16), spread)[0:1]
    diagonal = lax.broadcasted_iota(jnp.int32, (rows, rows), 0) == lax.broadcasted_iota(
        jnp.int32, (rows, rows), 1
    )
    ones = jnp.ones((rows, lanes), jnp.bfloat16)
    columns = []
    for h in range(halo, -1, -1):
        line = seg_ref[pl.ds(jnp.maximum(me - h, 0), 1), :].astype(jnp.float32)
        line = jnp.where(me >= h, line, -1.0)
        column = jnp.where(diagonal, jnp.broadcast_to(line, (rows, rows)), 0.0)
        columns.append(nn(column.astype(jnp.bfloat16), ones))
    seg_key = jnp.concatenate(columns, axis=0)
    key_row = lax.broadcasted_iota(jnp.int32, (width, lanes), 0)
    query_row = lax.broadcasted_iota(jnp.int32, (width, lanes), 1) // group
    causal = key_row <= query_row + span
    for a in range(parts):
        same = seg_key[a * SUB : a * SUB + width] == seg_query[:, a * lanes : (a + 1) * lanes]
        bias[a] = jnp.where(same & causal, 0.0, MASKED)

    def pair(jj, _):
        load(0, q_hbm, q_buf, jj).wait()
        load(1, g_hbm, g_buf, jj).wait()
        load(2, o_hbm, o_buf, jj).wait()
        for h in range(1, halo + 1):
            @pl.when(me >= h)
            def _():
                forward(h, jj).wait_recv()

        q_pair = q_buf[jj].astype(jnp.float32)
        g_pair = g_buf[jj].astype(jnp.float32)
        o_pair = o_buf[jj].astype(jnp.float32)
        dq_pair = []
        for c in range(2):
            heads = slice(c * group, (c + 1) * group)
            q = q_pair[:, heads, :].reshape(rows * group, dim).astype(jnp.bfloat16)
            g_wide = g_pair[:, heads, :].reshape(rows * group, dim)
            g = g_wide.astype(jnp.bfloat16)
            product = g_wide * o_pair[:, heads, :].reshape(rows * group, dim)
            high = product.astype(jnp.bfloat16)
            low = (product - high.astype(jnp.float32)).astype(jnp.bfloat16)
            one = jnp.ones((8, dim), jnp.bfloat16)
            delta = (nt(one, high) + nt(one, low))[0:1]
            k = jnp.concatenate(
                [kv_prev[h - 1, jj, 2 * c] for h in range(halo, 0, -1)] + [kv_own[jj, 2 * c]], axis=0
            )
            v = jnp.concatenate(
                [kv_prev[h - 1, jj, 2 * c + 1] for h in range(halo, 0, -1)] + [kv_own[jj, 2 * c + 1]],
                axis=0,
            )
            pieces = (span + rows) // SUB
            dk = [None] * pieces
            dv = [None] * pieces
            dq = []
            for a in range(parts):
                q_a = q[a * lanes : (a + 1) * lanes]
                g_a = g[a * lanes : (a + 1) * lanes]
                k_a = k[a * SUB : a * SUB + width]
                v_a = v[a * SUB : a * SUB + width]
                raw = nt(k_a, q_a) + bias[a]
                top = jnp.max(raw, axis=0, keepdims=True)
                e = jnp.exp2((raw - top) * (scale * math.log2(math.e)))
                prob = e * (1.0 / jnp.sum(e, axis=0, keepdims=True))
                d_prob = nt(v_a, g_a)
                d_score = (prob * (d_prob - delta[:, a * lanes : (a + 1) * lanes])).astype(jnp.bfloat16)
                dv_a = nn(prob.astype(jnp.bfloat16), g_a)
                dk_a = nn(d_score, q_a)
                dq.append(tn(d_score, k_a) * scale)
                for b in range(width // SUB):
                    at = slice(b * SUB, (b + 1) * SUB)
                    dk[a + b] = dk_a[at] if dk[a + b] is None else dk[a + b] + dk_a[at]
                    dv[a + b] = dv_a[at] if dv[a + b] is None else dv[a + b] + dv_a[at]
            dq_pair.append(jnp.concatenate(dq, axis=0).reshape(rows, group, dim))
            for h in range(halo, -1, -1):
                at = slice((halo - h) * parts, (halo - h + 1) * parts)
                dk_h = jnp.concatenate(dk[at], axis=0) * scale
                dv_h = jnp.concatenate(dv[at], axis=0)
                if h:
                    back_out[h - 1, jj, 2 * c] = dk_h.astype(jnp.bfloat16)
                    back_out[h - 1, jj, 2 * c + 1] = dv_h.astype(jnp.bfloat16)
                else:
                    own_sum[jj, 2 * c] = dk_h
                    own_sum[jj, 2 * c + 1] = dv_h
        dq_buf[jj] = jnp.concatenate(dq_pair, axis=1).astype(jnp.bfloat16)
        store(jj).start()
        for h in range(1, halo + 1):
            @pl.when(me >= h)
            def _():
                backward(h, jj).start()
        return 0

    lax.fori_loop(0, pairs, pair, 0)

    for jj in range(pairs):
        for h in range(1, halo + 1):
            @pl.when(me + h < devices)
            def _():
                backward(h, jj).wait_recv()
                own_sum[jj] = own_sum[jj] + back_in[h - 1, jj].astype(jnp.float32)
        for c in range(2):
            for which in range(2):
                flat[which, pl.ds(2 * jj + c, rows, stride=kv_heads), :] = own_sum[jj, 2 * c + which]
    dk_ref[...] = flat[0].reshape(rows, kv_heads, dim).astype(jnp.bfloat16)
    dv_ref[...] = flat[1].reshape(rows, kv_heads, dim).astype(jnp.bfloat16)

    for jj in range(pairs):
        store(jj).wait()
        for h in range(1, halo + 1):
            @pl.when(me + h < devices)
            def _():
                forward(h, jj).wait_send()

            @pl.when(me >= h)
            def _():
                backward(h, jj).wait_send()


def shards(queries, keys, values, outputs, out_grad, segments):
    ctx_count, head_count = lax.axis_size("ctx"), lax.axis_size("head")
    rows, q_heads, dim = queries.shape
    kv_heads = keys.shape[1]
    group = q_heads // kv_heads
    halo = max(1, head_count // 4)
    pairs = kv_heads // 2
    width = halo * rows + SUB
    sizes = (ctx_count, head_count, halo, rows, kv_heads, group, dim)
    lines = segments.reshape(ctx_count * head_count, rows)
    bf16, f32 = jnp.bfloat16, jnp.float32
    big = pltpu.VMEM((pairs, rows, 2 * group, dim), bf16)
    vmem = pl.BlockSpec(memory_space=pltpu.VMEM)
    hbm = pl.BlockSpec(memory_space=pl.ANY)
    work = rows * q_heads * (halo + 1) * rows
    return pl.pallas_call(
        functools.partial(kernel, sizes),
        out_shape=(
            jax.ShapeDtypeStruct(queries.shape, bf16),
            jax.ShapeDtypeStruct(keys.shape, bf16),
            jax.ShapeDtypeStruct(values.shape, bf16),
        ),
        in_specs=[hbm, vmem, vmem, hbm, hbm, vmem],
        out_specs=(hbm, vmem, vmem),
        scratch_shapes=[
            big, big, big, big,
            pltpu.VMEM((2, rows * kv_heads, dim), f32),
            pltpu.VMEM((pairs, 4, rows, dim), bf16),
            pltpu.VMEM((halo, pairs, 4, rows, dim), bf16),
            pltpu.VMEM((halo, pairs, 4, rows, dim), bf16),
            pltpu.VMEM((halo, pairs, 4, rows, dim), bf16),
            pltpu.VMEM((pairs, 4, rows, dim), f32),
            pltpu.VMEM((rows // SUB, width, SUB * group), f32),
            pltpu.SemaphoreType.DMA((3, pairs)),
            pltpu.SemaphoreType.DMA((pairs,)),
            pltpu.SemaphoreType.DMA((halo, pairs)),
            pltpu.SemaphoreType.DMA((halo, pairs)),
            pltpu.SemaphoreType.DMA((halo, pairs)),
            pltpu.SemaphoreType.DMA((halo, pairs)),
        ],
        compiler_params=pltpu.CompilerParams(
            collective_id=0, has_side_effects=True, vmem_limit_bytes=48 * 1024 * 1024
        ),
        cost_estimate=pl.CostEstimate(
            flops=10 * work * dim, bytes_accessed=8 * rows * q_heads * dim, transcendentals=work
        ),
    )(queries, keys, values, outputs, out_grad, lines)


def solution(mesh):
    tokens = P(("ctx", "head"), None, None)
    return jax.shard_map(
        shards,
        mesh=mesh,
        in_specs=(tokens, tokens, tokens, tokens, tokens, P()),
        out_specs=(tokens, tokens, tokens),
        check_vma=False,
    )
```

time: 199 us -> 31 us (0.16); the launches traced: 196 us -> 30.7 us
  waiting for transfers between devices: 50.9 us -> 0 us
  starting transfers between devices: 50.7 us -> 0 us
  matrix products: 47.5 us -> 0 us
  local copies, waits for them, and re-layouts: 32 us -> 6.93 us
  Pallas kernels: 0 us -> 23.1 us
  other arithmetic: 13.9 us -> 0 us
    dot_general x5 -> x0, matrix products: 47.5 us -> none  [the longest x1 13.3 us: heads_layout(): jnp.einsum('bkgd,wkd->kgbw', g_block, v_window, preferred_element_type=jn...]
    all_to_all x8 -> x0, waiting for transfers between devices: 44.7 us -> none  [the longest x1 22 us: heads_layout(): lax.all_to_all(query_local, 'head', split_axis=0, concat_axis=1, tiled=True)]
    all_to_all x8 -> x0, starting transfers between devices: 39 us -> none  [the longest x1 5.6 us: heads_layout(): lax.all_to_all(outputs, 'head', split_axis=1, concat_axis=0, tiled=True)]
    pallas_call x0 -> x1, Pallas kernels: none -> 23.1 us  [shards(): pl.pallas_call(functools.partial(kernel, sizes), out_shape=(jax.ShapeDtyp...]
    unnamed x19 -> x11, local copies, waits for them, and re-layouts: 19 us -> 6.93 us
    ppermute x4 -> x0, starting transfers between devices: 11.7 us -> none  [shifted(): return lax.ppermute(block, axis, route)]
    reduce_sum x2 -> x0, other arithmetic: 11.4 us -> none  [the longest x1 9.52 us: heads_layout(): jnp.sum(jnp.exp(masked - top[..., None]), axis=-1)]
    ppermute x4 -> x0, waiting for transfers between devices: 6.23 us -> none  [shifted(): return lax.ppermute(block, axis, route)]
  transfers between devices with their start and end apart: 12 -> 0, of which waited for: 6 -> 0; matrix products, arithmetic and copies ran while one was open for 44% -> 0% of each run, Pallas kernels for 0% -> 0%
where the time goes in v1:
time: 31 us; the launch traced here: 30.7 us
  Pallas kernels  23.1 us (75%)
  local copies, waits for them, and re-layouts  6.93 us (22%)
  between operations  0.65 us (2%)
    pallas_call x1, Pallas kernels, shards(): pl.pallas_call(functools.partial(kernel, sizes), out_shape=(jax.ShapeDtyp...  23.1 us
    unnamed x11, local copies, waits for them, and re-layouts  6.93 us

profile of v1, /device:TPU:15, one launch (start us, length us, event | category | flops | bytes accessed | tf_op | source)
XLA Modules:
  0.0 30.7 jit_solution(1595783803989128112)
XLA Ops:
  0.6 0.0 copy-start
  0.6 1.6 %copy-done = bf16[128,64,128]{2,1,0:T(8,128)(2,1)S(1)} copy-done((bf16[128,64,128]{2,1,0:T(8,128)(2,1)S(1)}, bf16[128,64,128]{2,1,0:T(8,128)(2,1)}, u32[]{:S(2)}) %copy-start) | copy-done | bytes 2097176
  2.2 0.0 copy-start.1
  2.2 0.9 %copy-done.1 = bf16[128,8,128]{2,1,0:T(8,128)(2,1)S(1)} copy-done((bf16[128,8,128]{2,1,0:T(8,128)(2,1)S(1)}, bf16[128,8,128]{2,1,0:T(8,128)(2,1)}, u32[]{:S(2)}) %copy-start.1) | copy-done | bytes 262168
  3.2 0.0 copy-start.2
  3.2 0.9 %copy-done.2 = bf16[128,8,128]{2,1,0:T(8,128)(2,1)S(1)} copy-done((bf16[128,8,128]{2,1,0:T(8,128)(2,1)S(1)}, bf16[128,8,128]{2,1,0:T(8,128)(2,1)}, u32[]{:S(2)}) %copy-start.2) | copy-done | bytes 262168
  4.1 0.0 copy-start.3
  4.1 0.7 %copy-done.3 = s32[4096]{0:T(1024)S(1)} copy-done((s32[4096]{0:T(1024)S(1)}, s32[4096]{0:T(1024)}, u32[]{:S(2)}) %copy-start.3) | copy-done | bytes 16408
  4.8 23.1 %shard_map.85 = (bf16[128,64,128]{2,1,0:T(8,128)(2,1)S(1)}, bf16[128,8,128]{2,1,0:T(8,128)(2,1)S(1)}, bf16[128,8,128]{2,1,0:T(8,128)(2,1)S(1)}) custom-call(bf16[128,64,128]{2,1,0:T(8,128)(2,1)S(1)} %copy-done, bf16[128,8,128]{2,1,0:T(8,128)(2,1)S(1)} %copy-done.1, bf16[128,8,128]{2,1,0:T(8,128)(2,1)S(1)} %copy-done.2, bf16[128,64,128]{2,1,0:T(8,128)(2,1)} %o_hbm.1, ...), custom_call_target="tpu_custom_call" | custom-call | flops 2684354560 | bytes 8388608 | tf_op jit(solution)/shard_map/pallas_call | solution.py:249
  28.0 1.3 %copy.12 = bf16[128,64,128]{2,1,0:T(8,128)(2,1)} copy(bf16[128,64,128]{2,1,0:T(8,128)(2,1)S(1)} %get-tuple-element.6) | data formatting | bytes 4194304
  29.3 0.7 %copy.13 = bf16[128,8,128]{2,1,0:T(8,128)(2,1)} copy(bf16[128,8,128]{2,1,0:T(8,128)(2,1)S(1)} %get-tuple-element.7) | data formatting | bytes 524288
  30.0 0.7 %copy.14 = bf16[128,8,128]{2,1,0:T(8,128)(2,1)} copy(bf16[128,8,128]{2,1,0:T(8,128)(2,1)S(1)} %get-tuple-element.8) | data formatting | bytes 524288
Async XLA Ops:
  0.6 1.6 %copy-start = (bf16[128,64,128]{2,1,0:T(8,128)(2,1)S(1)}, bf16[128,64,128]{2,1,0:T(8,128)(2,1)}, u32[]{:S(2)}) copy-start(bf16[128,64,128]{2,1,0:T(8,128)(2,1)} %q_hbm.1) | copy-start | bytes 6291460
  2.2 0.9 %copy-start.1 = (bf16[128,8,128]{2,1,0:T(8,128)(2,1)S(1)}, bf16[128,8,128]{2,1,0:T(8,128)(2,1)}, u32[]{:S(2)}) copy-start(bf16[128,8,128]{2,1,0:T(8,128)(2,1)} %k_ref.1) | copy-start | bytes 786436
  3.2 0.9 %copy-start.2 = (bf16[128,8,128]{2,1,0:T(8,128)(2,1)S(1)}, bf16[128,8,128]{2,1,0:T(8,128)(2,1)}, u32[]{:S(2)}) copy-start(bf16[128,8,128]{2,1,0:T(8,128)(2,1)} %v_ref.1) | copy-start | bytes 786436
  4.1 0.7 %copy-start.3 = (s32[4096]{0:T(1024)S(1)}, s32[4096]{0:T(1024)}, u32[]{:S(2)}) copy-start(s32[4096]{0:T(1024)} %param.11) | copy-start | bytes 49156

commit v2 on v1

--- a/solution.py
+++ b/solution.py
@@ -27,10 +27,10 @@
 
 def kernel(
     sizes,
-    q_hbm, k_ref, v_ref, o_hbm, g_hbm, seg_ref,
-    dq_hbm, dk_ref, dv_ref,
-    q_buf, g_buf, o_buf, dq_buf, flat, kv_own, kv_prev, back_out, back_in, own_sum, bias,
-    in_sem, dq_sem, fwd_send, fwd_recv, bwd_send, bwd_recv,
+    q_hbm, k_hbm, v_hbm, o_hbm, g_hbm, seg_hbm,
+    dq_hbm, dk_hbm, dv_hbm,
+    q_buf, g_buf, o_buf, dq_buf, kv_raw, seg_ref, flat, kv_own, kv_prev, back_out, back_in, own_sum, bias,
+    in_sem, dq_sem, kv_sem, fwd_send, fwd_recv, bwd_send, bwd_recv,
 ):
     ctx_count, head_count, halo, rows, kv_heads, group, dim = sizes
     devices = ctx_count * head_count
@@ -52,9 +52,7 @@
         )
 
     def store(jj):
-        return pltpu.make_async_copy(
-            dq_buf.at[jj], dq_hbm.at[:, pl.ds(jj * wide, wide), :], dq_sem.at[jj]
-        )
+        return pltpu.make_async_copy(dq_buf.at[jj], dq_hbm.at[jj], dq_sem.at[jj])
 
     def forward(h, jj):
         return pltpu.make_async_remote_copy(
@@ -70,6 +68,13 @@
             device_id=device(me - h), device_id_type=MESH,
         )
 
+    first = [
+        pltpu.make_async_copy(k_hbm, kv_raw.at[0], kv_sem.at[0]),
+        pltpu.make_async_copy(v_hbm, kv_raw.at[1], kv_sem.at[1]),
+        pltpu.make_async_copy(seg_hbm, seg_ref, kv_sem.at[2]),
+    ]
+    for copy in first:
+        copy.start()
     barrier = pltpu.get_barrier_semaphore()
     for h in range(1, halo + 1):
         @pl.when(me >= h)
@@ -85,8 +90,9 @@
         load(1, g_hbm, g_buf, jj).start()
         load(2, o_hbm, o_buf, jj).start()
 
-    flat[0] = k_ref[...].astype(jnp.float32).reshape(rows * kv_heads, dim)
-    flat[1] = v_ref[...].astype(jnp.float32).reshape(rows * kv_heads, dim)
+    for which in range(2):
+        first[which].wait()
+        flat[which] = kv_raw[which].astype(jnp.float32).reshape(rows * kv_heads, dim)
 
     def split(jj):
         for c in range(2):
@@ -111,6 +117,7 @@
         def _():
             kv_prev[h - 1] = jnp.zeros(kv_prev.shape[1:], kv_prev.dtype)
 
+    first[2].wait()
     token = lax.broadcasted_iota(jnp.int32, (rows, rows * group), 0)
     lane = lax.broadcasted_iota(jnp.int32, (rows, rows * group), 1)
     spread = jnp.where(lane // group == token, 1.0, 0.0).astype(jnp.bfloat16)
@@ -134,6 +141,8 @@
         same = seg_key[a * SUB : a * SUB + width] == seg_query[:, a * lanes : (a + 1) * lanes]
         bias[a] = jnp.where(same & causal, 0.0, MASKED)
 
+    low_half = lax.broadcasted_iota(jnp.int32, (rows * group, dim), 1) < dim // 2
+
     def pair(jj, _):
         load(0, q_hbm, q_buf, jj).wait()
         load(1, g_hbm, g_buf, jj).wait()
@@ -153,10 +162,10 @@
             g_wide = g_pair[:, heads, :].reshape(rows * group, dim)
             g = g_wide.astype(jnp.bfloat16)
             product = g_wide * o_pair[:, heads, :].reshape(rows * group, dim)
-            high = product.astype(jnp.bfloat16)
-            low = (product - high.astype(jnp.float32)).astype(jnp.bfloat16)
-            one = jnp.ones((8, dim), jnp.bfloat16)
-            delta = (nt(one, high) + nt(one, low))[0:1]
+            product = product + pltpu.roll(product, dim // 2, 1)
+            high = product.astype(jnp.bfloat16).astype(jnp.float32)
+            terms = jnp.where(low_half, high, product - high).astype(jnp.bfloat16)
+            g_terms = jnp.concatenate([g, terms], axis=1)
             k = jnp.concatenate(
                 [kv_prev[h - 1, jj, 2 * c] for h in range(halo, 0, -1)] + [kv_own[jj, 2 * c]], axis=0
             )
@@ -164,6 +173,7 @@
                 [kv_prev[h - 1, jj, 2 * c + 1] for h in range(halo, 0, -1)] + [kv_own[jj, 2 * c + 1]],
                 axis=0,
             )
+            v = jnp.concatenate([v, jnp.full(v.shape, -1.0, v.dtype)], axis=1)
             pieces = (span + rows) // SUB
             dk = [None] * pieces
             dv = [None] * pieces
@@ -177,8 +187,8 @@
                 top = jnp.max(raw, axis=0, keepdims=True)
                 e = jnp.exp2((raw - top) * (scale * math.log2(math.e)))
                 prob = e * (1.0 / jnp.sum(e, axis=0, keepdims=True))
-                d_prob = nt(v_a, g_a)
-                d_score = (prob * (d_prob - delta[:, a * lanes : (a + 1) * lanes])).astype(jnp.bfloat16)
+                d_prob = nt(v_a, g_terms[a * lanes : (a + 1) * lanes])
+                d_score = (prob * d_prob).astype(jnp.bfloat16)
                 dv_a = nn(prob.astype(jnp.bfloat16), g_a)
                 dk_a = nn(d_score, q_a)
                 dq.append(tn(d_score, k_a) * scale)
@@ -216,8 +226,13 @@
         for c in range(2):
             for which in range(2):
                 flat[which, pl.ds(2 * jj + c, rows, stride=kv_heads), :] = own_sum[jj, 2 * c + which]
-    dk_ref[...] = flat[0].reshape(rows, kv_heads, dim).astype(jnp.bfloat16)
-    dv_ref[...] = flat[1].reshape(rows, kv_heads, dim).astype(jnp.bfloat16)
+    last = [
+        pltpu.make_async_copy(kv_raw.at[0], dk_hbm, kv_sem.at[0]),
+        pltpu.make_async_copy(kv_raw.at[1], dv_hbm, kv_sem.at[1]),
+    ]
+    for which in range(2):
+        kv_raw[which] = flat[which].reshape(rows, kv_heads, dim).astype(jnp.bfloat16)
+        last[which].start()
 
     for jj in range(pairs):
         store(jj).wait()
@@ -229,6 +244,22 @@
             @pl.when(me >= h)
             def _():
                 backward(h, jj).wait_send()
+    for copy in last:
+        copy.wait()
+
+
+def write(dq_ref, dk_ref, dv_ref, dq_hbm, dk_hbm, dv_hbm, sem):
+    pairs, _, wide, _ = dq_ref.shape
+    copies = [
+        pltpu.make_async_copy(dq_ref.at[jj], dq_hbm.at[:, pl.ds(jj * wide, wide), :], sem.at[jj])
+        for jj in range(pairs)
+    ]
+    copies.append(pltpu.make_async_copy(dk_ref, dk_hbm, sem.at[pairs]))
+    copies.append(pltpu.make_async_copy(dv_ref, dv_hbm, sem.at[pairs + 1]))
+    for copy in copies:
+        copy.start()
+    for copy in copies:
+        copy.wait()
 
 
 def shards(queries, keys, values, outputs, out_grad, segments):
@@ -243,20 +274,27 @@
     lines = segments.reshape(ctx_count * head_count, rows)
     bf16, f32 = jnp.bfloat16, jnp.float32
     big = pltpu.VMEM((pairs, rows, 2 * group, dim), bf16)
-    vmem = pl.BlockSpec(memory_space=pltpu.VMEM)
     hbm = pl.BlockSpec(memory_space=pl.ANY)
+    limit = 56 * 1024 * 1024
     work = rows * q_heads * (halo + 1) * rows
-    return pl.pallas_call(
+    shapes = (
+        jax.ShapeDtypeStruct(queries.shape, bf16),
+        jax.ShapeDtypeStruct(keys.shape, bf16),
+        jax.ShapeDtypeStruct(values.shape, bf16),
+    )
+    grads = pl.pallas_call(
         functools.partial(kernel, sizes),
         out_shape=(
-            jax.ShapeDtypeStruct(queries.shape, bf16),
+            jax.ShapeDtypeStruct((pairs, rows, 2 * group, dim), bf16),
             jax.ShapeDtypeStruct(keys.shape, bf16),
             jax.ShapeDtypeStruct(values.shape, bf16),
         ),
-        in_specs=[hbm, vmem, vmem, hbm, hbm, vmem],
-        out_specs=(hbm, vmem, vmem),
+        in_specs=[hbm] * 6,
+        out_specs=(hbm,) * 3,
         scratch_shapes=[
             big, big, big, big,
+            pltpu.VMEM((2, rows, kv_heads, dim), bf16),
+            pltpu.VMEM(lines.shape, jnp.int32),
             pltpu.VMEM((2, rows * kv_heads, dim), f32),
             pltpu.VMEM((pairs, 4, rows, dim), bf16),
             pltpu.VMEM((halo, pairs, 4, rows, dim), bf16),
@@ -266,18 +304,27 @@
             pltpu.VMEM((rows // SUB, width, SUB * group), f32),
             pltpu.SemaphoreType.DMA((3, pairs)),
             pltpu.SemaphoreType.DMA((pairs,)),
+            pltpu.SemaphoreType.DMA((3,)),
             pltpu.SemaphoreType.DMA((halo, pairs)),
             pltpu.SemaphoreType.DMA((halo, pairs)),
             pltpu.SemaphoreType.DMA((halo, pairs)),
             pltpu.SemaphoreType.DMA((halo, pairs)),
         ],
         compiler_params=pltpu.CompilerParams(
-            collective_id=0, has_side_effects=True, vmem_limit_bytes=48 * 1024 * 1024
+            collective_id=0, has_side_effects=True, vmem_limit_bytes=limit
         ),
         cost_estimate=pl.CostEstimate(
             flops=10 * work * dim, bytes_accessed=8 * rows * q_heads * dim, transcendentals=work
         ),
     )(queries, keys, values, outputs, out_grad, lines)
+    return pl.pallas_call(
+        write,
+        out_shape=shapes,
+        in_specs=[hbm] * 3,
+        out_specs=(hbm,) * 3,
+        scratch_shapes=[pltpu.SemaphoreType.DMA((pairs + 2,))],
+        compiler_params=pltpu.CompilerParams(vmem_limit_bytes=limit),
+    )(*grads)
 
 
 def solution(mesh):

time: 31 us -> 104 us (3.35)
  Pallas kernels: 23.1 us -> 103 us
  local copies, waits for them, and re-layouts: 6.93 us -> 0 us
    pallas_call x0 -> x1, Pallas kernels: none -> 80.6 us  [shards(): pl.pallas_call(write, out_shape=shapes, in_specs=[hbm] * 3, out_specs=(hb...]
    unnamed x11 -> x0, local copies, waits for them, and re-layouts: 6.93 us -> none
where the time goes in v2:
time: 104 us
  Pallas kernels  103 us (99%)
    pallas_call x1, Pallas kernels, shards(): pl.pallas_call(write, out_shape=shapes, in_specs=[hbm] * 3, out_specs=(hb...  80.6 us
    pallas_call x1, Pallas kernels, shards(): pl.pallas_call(functools.partial(kernel, sizes), out_shape=(jax.ShapeDtyp...  22.4 us

profile of v2, /device:TPU:15, one launch (start us, length us, event | category | flops | bytes accessed | tf_op | source)
XLA Modules:
  0.0 103.6 jit_solution(6569133394590060578)
XLA Ops:
  0.6 22.4 %shard_map.85 = (bf16[4,128,16,128]{3,2,1,0:T(8,128)(2,1)}, bf16[128,8,128]{2,1,0:T(8,128)(2,1)}, bf16[128,8,128]{2,1,0:T(8,128)(2,1)}) custom-call(bf16[128,64,128]{2,1,0:T(8,128)(2,1)} %q_hbm.1, bf16[128,8,128]{2,1,0:T(8,128)(2,1)} %k_hbm.1, bf16[128,8,128]{2,1,0:T(8,128)(2,1)} %v_hbm.1, bf16[128,64,128]{2,1,0:T(8,128)(2,1)} %o_hbm.1, ...), custom_call_target="tpu_custom_call" | custom-call | flops 2684354560 | bytes 8388608 | tf_op jit(solution)/shard_map/pallas_call | solution.py:285
  23.1 80.6 %shard_map.86 = (bf16[128,64,128]{2,1,0:T(8,128)(2,1)}, bf16[128,8,128]{2,1,0:T(8,128)(2,1)}, bf16[128,8,128]{2,1,0:T(8,128)(2,1)}) custom-call(bf16[4,128,16,128]{3,2,1,0:T(8,128)(2,1)} %get-tuple-element.6.dq_ref, bf16[128,8,128]{2,1,0:T(8,128)(2,1)} %get-tuple-element.7.dk_ref, bf16[128,8,128]{2,1,0:T(8,128)(2,1)} %get-tuple-element.8.dv_ref), custom_call_target="tpu_custom_call" | custom-call | tf_op jit(solution)/shard_map/pallas_call | solution.py:320

commit v3 on v2

--- a/solution.py
+++ b/solution.py
@@ -9,6 +9,7 @@
 from jax.sharding import PartitionSpec as P
 
 SUB = 32
+PARTS = 8
 MASKED = -1e30
 MESH = pl.DeviceIdType.MESH
 
@@ -52,7 +53,9 @@
         )
 
     def store(jj):
-        return pltpu.make_async_copy(dq_buf.at[jj], dq_hbm.at[jj], dq_sem.at[jj])
+        return pltpu.make_async_copy(
+            dq_buf.at[jj], dq_hbm.at[:, pl.ds(jj * wide, wide), :], dq_sem.at[jj]
+        )
 
     def forward(h, jj):
         return pltpu.make_async_remote_copy(
@@ -248,17 +251,23 @@
         copy.wait()
 
 
-def write(dq_ref, dk_ref, dv_ref, dq_hbm, dk_hbm, dv_hbm, sem):
-    pairs, _, wide, _ = dq_ref.shape
-    copies = [
-        pltpu.make_async_copy(dq_ref.at[jj], dq_hbm.at[:, pl.ds(jj * wide, wide), :], sem.at[jj])
-        for jj in range(pairs)
+def write(dq_in, dk_in, dv_in, dq_out, dk_out, dv_out, dq_buf, kv_buf, in_sem, out_sem):
+    rows = dq_in.shape[0]
+    step = rows // PARTS
+    routes = [
+        (dq_in.at[pl.ds(c * step, step)], dq_buf.at[pl.ds(c * step, step)], dq_out.at[pl.ds(c * step, step)])
+        for c in range(PARTS)
     ]
-    copies.append(pltpu.make_async_copy(dk_ref, dk_hbm, sem.at[pairs]))
-    copies.append(pltpu.make_async_copy(dv_ref, dv_hbm, sem.at[pairs + 1]))
-    for copy in copies:
+    routes.append((dk_in, kv_buf.at[0], dk_out))
+    routes.append((dv_in, kv_buf.at[1], dv_out))
+    loads = [pltpu.make_async_copy(a, b, in_sem.at[n]) for n, (a, b, _) in enumerate(routes)]
+    stores = [pltpu.make_async_copy(b, c, out_sem.at[n]) for n, (_, b, c) in enumerate(routes)]
+    for copy in loads:
         copy.start()
-    for copy in copies:
+    for load, store in zip(loads, stores):
+        load.wait()
+        store.start()
+    for copy in stores:
         copy.wait()
 
 
@@ -284,11 +293,7 @@
     )
     grads = pl.pallas_call(
         functools.partial(kernel, sizes),
-        out_shape=(
-            jax.ShapeDtypeStruct((pairs, rows, 2 * group, dim), bf16),
-            jax.ShapeDtypeStruct(keys.shape, bf16),
-            jax.ShapeDtypeStruct(values.shape, bf16),
-        ),
+        out_shape=shapes,
         in_specs=[hbm] * 6,
         out_specs=(hbm,) * 3,
         scratch_shapes=[
@@ -322,7 +327,12 @@
         out_shape=shapes,
         in_specs=[hbm] * 3,
         out_specs=(hbm,) * 3,
-        scratch_shapes=[pltpu.SemaphoreType.DMA((pairs + 2,))],
+        scratch_shapes=[
+            pltpu.VMEM(queries.shape, bf16),
+            pltpu.VMEM((2, *keys.shape), bf16),
+            pltpu.SemaphoreType.DMA((PARTS + 2,)),
+            pltpu.SemaphoreType.DMA((PARTS + 2,)),
+        ],
         compiler_params=pltpu.CompilerParams(vmem_limit_bytes=limit),
     )(*grads)
 

time: 104 us -> 25.8 us (0.25)
  Pallas kernels: 103 us -> 25 us
    pallas_call x1, Pallas kernels: 80.6 us -> 2.6 us  [shards(): pl.pallas_call(write, out_shape=shapes, in_specs=[hbm] * 3, out_specs=(hb...]
where the time goes in v3:
time: 25.8 us; the launch traced here: 25.7 us
  Pallas kernels  25 us (97%)
  between operations  0.64 us (2%)
    pallas_call x1, Pallas kernels, shards(): pl.pallas_call(functools.partial(kernel, sizes), out_shape=shapes, in_spe...  22.4 us
    pallas_call x1, Pallas kernels, shards(): pl.pallas_call(write, out_shape=shapes, in_specs=[hbm] * 3, out_specs=(hb...  2.6 us

profile of v3, /device:TPU:15, one launch (start us, length us, event | category | flops | bytes accessed | tf_op | source)
XLA Modules:
  0.0 25.7 jit_solution(14734611930338801684)
XLA Ops:
  0.6 22.4 %shard_map.85 = (bf16[128,64,128]{2,1,0:T(8,128)(2,1)}, bf16[128,8,128]{2,1,0:T(8,128)(2,1)}, bf16[128,8,128]{2,1,0:T(8,128)(2,1)}) custom-call(bf16[128,64,128]{2,1,0:T(8,128)(2,1)} %q_hbm.1, bf16[128,8,128]{2,1,0:T(8,128)(2,1)} %k_hbm.1, bf16[128,8,128]{2,1,0:T(8,128)(2,1)} %v_hbm.1, bf16[128,64,128]{2,1,0:T(8,128)(2,1)} %o_hbm.1, ...), custom_call_target="tpu_custom_call" | custom-call | flops 2684354560 | bytes 8388608 | tf_op jit(solution)/shard_map/pallas_call | solution.py:294
  23.1 2.6 %shard_map.86 = (bf16[128,64,128]{2,1,0:T(8,128)(2,1)}, bf16[128,8,128]{2,1,0:T(8,128)(2,1)}, bf16[128,8,128]{2,1,0:T(8,128)(2,1)}) custom-call(bf16[128,64,128]{2,1,0:T(8,128)(2,1)} %get-tuple-element.6.dq_in, bf16[128,8,128]{2,1,0:T(8,128)(2,1)} %get-tuple-element.7.dk_in, bf16[128,8,128]{2,1,0:T(8,128)(2,1)} %get-tuple-element.8.dv_in), custom_call_target="tpu_custom_call" | custom-call | tf_op jit(solution)/shard_map/pallas_call | solution.py:325

commit v4 on v3

--- a/solution.py
+++ b/solution.py
@@ -30,7 +30,7 @@
     sizes,
     q_hbm, k_hbm, v_hbm, o_hbm, g_hbm, seg_hbm,
     dq_hbm, dk_hbm, dv_hbm,
-    q_buf, g_buf, o_buf, dq_buf, kv_raw, seg_ref, flat, kv_own, kv_prev, back_out, back_in, own_sum, bias,
+    q_buf, g_buf, o_buf, dq_buf, q_rows, g_rows, kv_raw, seg_ref, flat, kv_own, kv_prev, back_out, back_in, own_sum, bias,
     in_sem, dq_sem, kv_sem, fwd_send, fwd_recv, bwd_send, bwd_recv,
 ):
     ctx_count, head_count, halo, rows, kv_heads, group, dim = sizes
@@ -146,29 +146,39 @@
 
     low_half = lax.broadcasted_iota(jnp.int32, (rows * group, dim), 1) < dim // 2
 
-    def pair(jj, _):
+    def prepare(jj, _):
         load(0, q_hbm, q_buf, jj).wait()
         load(1, g_hbm, g_buf, jj).wait()
         load(2, o_hbm, o_buf, jj).wait()
-        for h in range(1, halo + 1):
-            @pl.when(me >= h)
-            def _():
-                forward(h, jj).wait_recv()
-
         q_pair = q_buf[jj].astype(jnp.float32)
         g_pair = g_buf[jj].astype(jnp.float32)
         o_pair = o_buf[jj].astype(jnp.float32)
-        dq_pair = []
         for c in range(2):
             heads = slice(c * group, (c + 1) * group)
-            q = q_pair[:, heads, :].reshape(rows * group, dim).astype(jnp.bfloat16)
+            q_wide = q_pair[:, heads, :].reshape(rows * group, dim)
             g_wide = g_pair[:, heads, :].reshape(rows * group, dim)
-            g = g_wide.astype(jnp.bfloat16)
             product = g_wide * o_pair[:, heads, :].reshape(rows * group, dim)
             product = product + pltpu.roll(product, dim // 2, 1)
             high = product.astype(jnp.bfloat16).astype(jnp.float32)
-            terms = jnp.where(low_half, high, product - high).astype(jnp.bfloat16)
-            g_terms = jnp.concatenate([g, terms], axis=1)
+            terms = jnp.where(low_half, high, product - high)
+            q_rows[2 * jj + c] = q_wide.astype(jnp.bfloat16)
+            g_rows[2 * jj + c, :, :dim] = g_wide.astype(jnp.bfloat16)
+            g_rows[2 * jj + c, :, dim:] = terms.astype(jnp.bfloat16)
+        return 0
+
+    lax.fori_loop(0, pairs, prepare, 0)
+
+    def pair(jj, _):
+        for h in range(1, halo + 1):
+            @pl.when(me >= h)
+            def _():
+                forward(h, jj).wait_recv()
+
+        dq_pair = []
+        for c in range(2):
+            q = q_rows[2 * jj + c]
+            g_terms = g_rows[2 * jj + c]
+            g = g_terms[:, :dim]
             k = jnp.concatenate(
                 [kv_prev[h - 1, jj, 2 * c] for h in range(halo, 0, -1)] + [kv_own[jj, 2 * c]], axis=0
             )
@@ -298,6 +308,8 @@
         out_specs=(hbm,) * 3,
         scratch_shapes=[
             big, big, big, big,
+            pltpu.VMEM((kv_heads, rows * group, dim), bf16),
+            pltpu.VMEM((kv_heads, rows * group, 2 * dim), bf16),
             pltpu.VMEM((2, rows, kv_heads, dim), bf16),
             pltpu.VMEM(lines.shape, jnp.int32),
             pltpu.VMEM((2, rows * kv_heads, dim), f32),

time: 25.8 us -> 25.8 us (level)
  no operation moved by 1% of the time
where the time goes in v4:
time: 25.8 us; the launch traced here: 25.7 us
  Pallas kernels  25 us (97%)
  between operations  0.64 us (2%)
    pallas_call x1, Pallas kernels, shards(): pl.pallas_call(functools.partial(kernel, sizes), out_shape=shapes, in_spe...  22.4 us
    pallas_call x1, Pallas kernels, shards(): pl.pallas_call(write, out_shape=shapes, in_specs=[hbm] * 3, out_specs=(hb...  2.6 us

profile of v4, /device:TPU:15, one launch (start us, length us, event | category | flops | bytes accessed | tf_op | source)
XLA Modules:
  0.0 25.7 jit_solution(16349107364617577751)
XLA Ops:
  0.6 22.4 %shard_map.85 = (bf16[128,64,128]{2,1,0:T(8,128)(2,1)}, bf16[128,8,128]{2,1,0:T(8,128)(2,1)}, bf16[128,8,128]{2,1,0:T(8,128)(2,1)}) custom-call(bf16[128,64,128]{2,1,0:T(8,128)(2,1)} %q_hbm.1, bf16[128,8,128]{2,1,0:T(8,128)(2,1)} %k_hbm.1, bf16[128,8,128]{2,1,0:T(8,128)(2,1)} %v_hbm.1, bf16[128,64,128]{2,1,0:T(8,128)(2,1)} %o_hbm.1, ...), custom_call_target="tpu_custom_call" | custom-call | flops 2684354560 | bytes 8388608 | tf_op jit(solution)/shard_map/pallas_call | solution.py:304
  23.1 2.6 %shard_map.86 = (bf16[128,64,128]{2,1,0:T(8,128)(2,1)}, bf16[128,8,128]{2,1,0:T(8,128)(2,1)}, bf16[128,8,128]{2,1,0:T(8,128)(2,1)}) custom-call(bf16[128,64,128]{2,1,0:T(8,128)(2,1)} %get-tuple-element.6.dq_in, bf16[128,8,128]{2,1,0:T(8,128)(2,1)} %get-tuple-element.7.dk_in, bf16[128,8,128]{2,1,0:T(8,128)(2,1)} %get-tuple-element.8.dv_in), custom_call_target="tpu_custom_call" | custom-call | tf_op jit(solution)/shard_map/pallas_call | solution.py:337

commit v5 on v4

--- a/solution.py
+++ b/solution.py
@@ -57,17 +57,17 @@
             dq_buf.at[jj], dq_hbm.at[:, pl.ds(jj * wide, wide), :], dq_sem.at[jj]
         )
 
-    def forward(h, jj):
+    def forward(h, j):
         return pltpu.make_async_remote_copy(
-            src_ref=kv_own.at[jj], dst_ref=kv_prev.at[h - 1, jj],
-            send_sem=fwd_send.at[h - 1, jj], recv_sem=fwd_recv.at[h - 1, jj],
+            src_ref=kv_own.at[j], dst_ref=kv_prev.at[h - 1, j],
+            send_sem=fwd_send.at[h - 1, j], recv_sem=fwd_recv.at[h - 1, j],
             device_id=device(me + h), device_id_type=MESH,
         )
 
-    def backward(h, jj):
+    def backward(h, j):
         return pltpu.make_async_remote_copy(
-            src_ref=back_out.at[h - 1, jj], dst_ref=back_in.at[h - 1, jj],
-            send_sem=bwd_send.at[h - 1, jj], recv_sem=bwd_recv.at[h - 1, jj],
+            src_ref=back_out.at[h - 1, j], dst_ref=back_in.at[h - 1, j],
+            send_sem=bwd_send.at[h - 1, j], recv_sem=bwd_recv.at[h - 1, j],
             device_id=device(me - h), device_id_type=MESH,
         )
 
@@ -97,23 +97,20 @@
         first[which].wait()
         flat[which] = kv_raw[which].astype(jnp.float32).reshape(rows * kv_heads, dim)
 
-    def split(jj):
-        for c in range(2):
-            for which in range(2):
-                kv_own[jj, 2 * c + which] = flat[
-                    which, pl.ds(2 * jj + c, rows, stride=kv_heads), :
-                ].astype(jnp.bfloat16)
+    def split(j):
+        for which in range(2):
+            kv_own[j, which] = flat[which, pl.ds(j, rows, stride=kv_heads), :].astype(jnp.bfloat16)
 
     split(0)
     pl.semaphore_wait(barrier, jnp.minimum(me, halo) + jnp.minimum(devices - 1 - me, halo))
 
-    for jj in range(pairs):
-        if jj:
-            split(jj)
+    for j in range(kv_heads):
+        if j:
+            split(j)
         for h in range(1, halo + 1):
             @pl.when(me + h < devices)
             def _():
-                forward(h, jj).start()
+                forward(h, j).start()
 
     for h in range(1, halo + 1):
         @pl.when(me < h)
@@ -169,23 +166,19 @@
     lax.fori_loop(0, pairs, prepare, 0)
 
     def pair(jj, _):
-        for h in range(1, halo + 1):
-            @pl.when(me >= h)
-            def _():
-                forward(h, jj).wait_recv()
-
         dq_pair = []
         for c in range(2):
-            q = q_rows[2 * jj + c]
-            g_terms = g_rows[2 * jj + c]
+            j = 2 * jj + c
+            for h in range(1, halo + 1):
+                @pl.when(me >= h)
+                def _():
+                    forward(h, j).wait_recv()
+
+            q = q_rows[j]
+            g_terms = g_rows[j]
             g = g_terms[:, :dim]
-            k = jnp.concatenate(
-                [kv_prev[h - 1, jj, 2 * c] for h in range(halo, 0, -1)] + [kv_own[jj, 2 * c]], axis=0
-            )
-            v = jnp.concatenate(
-                [kv_prev[h - 1, jj, 2 * c + 1] for h in range(halo, 0, -1)] + [kv_own[jj, 2 * c + 1]],
-                axis=0,
-            )
+            k = jnp.concatenate([kv_prev[h - 1, j, 0] for h in range(halo, 0, -1)] + [kv_own[j, 0]], axis=0)
+            v = jnp.concatenate([kv_prev[h - 1, j, 1] for h in range(halo, 0, -1)] + [kv_own[j, 1]], axis=0)
             v = jnp.concatenate([v, jnp.full(v.shape, -1.0, v.dtype)], axis=1)
             pieces = (span + rows) // SUB
             dk = [None] * pieces
@@ -215,30 +208,29 @@
                 dk_h = jnp.concatenate(dk[at], axis=0) * scale
                 dv_h = jnp.concatenate(dv[at], axis=0)
                 if h:
-                    back_out[h - 1, jj, 2 * c] = dk_h.astype(jnp.bfloat16)
-                    back_out[h - 1, jj, 2 * c + 1] = dv_h.astype(jnp.bfloat16)
+                    back_out[h - 1, j, 0] = dk_h.astype(jnp.bfloat16)
+                    back_out[h - 1, j, 1] = dv_h.astype(jnp.bfloat16)
                 else:
-                    own_sum[jj, 2 * c] = dk_h
-                    own_sum[jj, 2 * c + 1] = dv_h
+                    own_sum[j, 0] = dk_h
+                    own_sum[j, 1] = dv_h
+            for h in range(1, halo + 1):
+                @pl.when(me >= h)
+                def _():
+                    backward(h, j).start()
         dq_buf[jj] = jnp.concatenate(dq_pair, axis=1).astype(jnp.bfloat16)
         store(jj).start()
-        for h in range(1, halo + 1):
-            @pl.when(me >= h)
-            def _():
-                backward(h, jj).start()
         return 0
 
     lax.fori_loop(0, pairs, pair, 0)
 
-    for jj in range(pairs):
+    for j in range(kv_heads):
         for h in range(1, halo + 1):
             @pl.when(me + h < devices)
             def _():
-                backward(h, jj).wait_recv()
-                own_sum[jj] = own_sum[jj] + back_in[h - 1, jj].astype(jnp.float32)
-        for c in range(2):
-            for which in range(2):
-                flat[which, pl.ds(2 * jj + c, rows, stride=kv_heads), :] = own_sum[jj, 2 * c + which]
+                backward(h, j).wait_recv()
+                own_sum[j] = own_sum[j] + back_in[h - 1, j].astype(jnp.float32)
+        for which in range(2):
+            flat[which, pl.ds(j, rows, stride=kv_heads), :] = own_sum[j, which]
     last = [
         pltpu.make_async_copy(kv_raw.at[0], dk_hbm, kv_sem.at[0]),
         pltpu.make_async_copy(kv_raw.at[1], dv_hbm, kv_sem.at[1]),
@@ -249,14 +241,15 @@
 
     for jj in range(pairs):
         store(jj).wait()
+    for j in range(kv_heads):
         for h in range(1, halo + 1):
             @pl.when(me + h < devices)
             def _():
-                forward(h, jj).wait_send()
+                forward(h, j).wait_send()
 
             @pl.when(me >= h)
             def _():
-                backward(h, jj).wait_send()
+                backward(h, j).wait_send()
     for copy in last:
         copy.wait()
 
@@ -313,19 +306,19 @@
             pltpu.VMEM((2, rows, kv_heads, dim), bf16),
             pltpu.VMEM(lines.shape, jnp.int32),
             pltpu.VMEM((2, rows * kv_heads, dim), f32),
-            pltpu.VMEM((pairs, 4, rows, dim), bf16),
-            pltpu.VMEM((halo, pairs, 4, rows, dim), bf16),
-            pltpu.VMEM((halo, pairs, 4, rows, dim), bf16),
-            pltpu.VMEM((halo, pairs, 4, rows, dim), bf16),
-            pltpu.VMEM((pairs, 4, rows, dim), f32),
+            pltpu.VMEM((kv_heads, 2, rows, dim), bf16),
+            pltpu.VMEM((halo, kv_heads, 2, rows, dim), bf16),
+            pltpu.VMEM((halo, kv_heads, 2, rows, dim), bf16),
+            pltpu.VMEM((halo, kv_heads, 2, rows, dim), bf16),
+            pltpu.VMEM((kv_heads, 2, rows, dim), f32),
             pltpu.VMEM((rows // SUB, width, SUB * group), f32),
             pltpu.SemaphoreType.DMA((3, pairs)),
             pltpu.SemaphoreType.DMA((pairs,)),
             pltpu.SemaphoreType.DMA((3,)),
-            pltpu.SemaphoreType.DMA((halo, pairs)),
-            pltpu.SemaphoreType.DMA((halo, pairs)),
-            pltpu.SemaphoreType.DMA((halo, pairs)),
-            pltpu.SemaphoreType.DMA((halo, pairs)),
+            pltpu.SemaphoreType.DMA((halo, kv_heads)),
+            pltpu.SemaphoreType.DMA((halo, kv_heads)),
+            pltpu.SemaphoreType.DMA((halo, kv_heads)),
+            pltpu.SemaphoreType.DMA((halo, kv_heads)),
         ],
         compiler_params=pltpu.CompilerParams(
             collective_id=0, has_side_effects=True, vmem_limit_bytes=limit

time: 25.8 us -> 25.3 us (0.981)
  Pallas kernels: 25 us -> 24.5 us
    pallas_call x1, Pallas kernels: 22.4 us -> 21.9 us  [shards(): pl.pallas_call(functools.partial(kernel, sizes), out_shape=shapes, in_spe...]
where the time goes in v5:
time: 25.3 us; the launch traced here: 25.2 us
  Pallas kernels  24.5 us (97%)
  between operations  0.64 us (3%)
    pallas_call x1, Pallas kernels, shards(): pl.pallas_call(functools.partial(kernel, sizes), out_shape=shapes, in_spe...  21.9 us
    pallas_call x1, Pallas kernels, shards(): pl.pallas_call(write, out_shape=shapes, in_specs=[hbm] * 3, out_specs=(hb...  2.6 us

profile of v5, /device:TPU:15, one launch (start us, length us, event | category | flops | bytes accessed | tf_op | source)
XLA Modules:
  0.0 25.2 jit_solution(18244533166682920012)
XLA Ops:
  0.6 21.9 %shard_map.85 = (bf16[128,64,128]{2,1,0:T(8,128)(2,1)}, bf16[128,8,128]{2,1,0:T(8,128)(2,1)}, bf16[128,8,128]{2,1,0:T(8,128)(2,1)}) custom-call(bf16[128,64,128]{2,1,0:T(8,128)(2,1)} %q_hbm.1, bf16[128,8,128]{2,1,0:T(8,128)(2,1)} %k_hbm.1, bf16[128,8,128]{2,1,0:T(8,128)(2,1)} %v_hbm.1, bf16[128,64,128]{2,1,0:T(8,128)(2,1)} %o_hbm.1, ...), custom_call_target="tpu_custom_call" | custom-call | flops 2684354560 | bytes 8388608 | tf_op jit(solution)/shard_map/pallas_call | solution.py:297
  22.6 2.6 %shard_map.86 = (bf16[128,64,128]{2,1,0:T(8,128)(2,1)}, bf16[128,8,128]{2,1,0:T(8,128)(2,1)}, bf16[128,8,128]{2,1,0:T(8,128)(2,1)}) custom-call(bf16[128,64,128]{2,1,0:T(8,128)(2,1)} %get-tuple-element.6.dq_in, bf16[128,8,128]{2,1,0:T(8,128)(2,1)} %get-tuple-element.7.dk_in, bf16[128,8,128]{2,1,0:T(8,128)(2,1)} %get-tuple-element.8.dv_in), custom_call_target="tpu_custom_call" | custom-call | tf_op jit(solution)/shard_map/pallas_call | solution.py:330

commit v6 on v5

--- a/solution.py
+++ b/solution.py
@@ -8,7 +8,7 @@
 from jax.experimental.pallas import tpu as pltpu
 from jax.sharding import PartitionSpec as P
 
-SUB = 32
+SUB = 64
 PARTS = 8
 MASKED = -1e30
 MESH = pl.DeviceIdType.MESH

time: 25.3 us -> 22.3 us (0.88)
  Pallas kernels: 24.5 us -> 21.5 us
    pallas_call x1, Pallas kernels: 21.9 us -> 18.9 us  [shards(): pl.pallas_call(functools.partial(kernel, sizes), out_shape=shapes, in_spe...]
where the time goes in v6:
time: 22.3 us; the launch traced here: 22.1 us
  Pallas kernels  21.5 us (96%)
  between operations  0.64 us (3%)
    pallas_call x1, Pallas kernels, shards(): pl.pallas_call(functools.partial(kernel, sizes), out_shape=shapes, in_spe...  18.9 us
    pallas_call x1, Pallas kernels, shards(): pl.pallas_call(write, out_shape=shapes, in_specs=[hbm] * 3, out_specs=(hb...  2.6 us

profile of v6, /device:TPU:15, one launch (start us, length us, event | category | flops | bytes accessed | tf_op | source)
XLA Modules:
  0.0 22.1 jit_solution(16366502426655643977)
XLA Ops:
  0.6 18.9 %shard_map.85 = (bf16[128,64,128]{2,1,0:T(8,128)(2,1)}, bf16[128,8,128]{2,1,0:T(8,128)(2,1)}, bf16[128,8,128]{2,1,0:T(8,128)(2,1)}) custom-call(bf16[128,64,128]{2,1,0:T(8,128)(2,1)} %q_hbm.1, bf16[128,8,128]{2,1,0:T(8,128)(2,1)} %k_hbm.1, bf16[128,8,128]{2,1,0:T(8,128)(2,1)} %v_hbm.1, bf16[128,64,128]{2,1,0:T(8,128)(2,1)} %o_hbm.1, ...), custom_call_target="tpu_custom_call" | custom-call | flops 2684354560 | bytes 8388608 | tf_op jit(solution)/shard_map/pallas_call | solution.py:297
  19.5 2.6 %shard_map.86 = (bf16[128,64,128]{2,1,0:T(8,128)(2,1)}, bf16[128,8,128]{2,1,0:T(8,128)(2,1)}, bf16[128,8,128]{2,1,0:T(8,128)(2,1)}) custom-call(bf16[128,64,128]{2,1,0:T(8,128)(2,1)} %get-tuple-element.6.dq_in, bf16[128,8,128]{2,1,0:T(8,128)(2,1)} %get-tuple-element.7.dk_in, bf16[128,8,128]{2,1,0:T(8,128)(2,1)} %get-tuple-element.8.dv_in), custom_call_target="tpu_custom_call" | custom-call | tf_op jit(solution)/shard_map/pallas_call | solution.py:330

commit v7 on v6

--- a/solution.py
+++ b/solution.py
@@ -8,7 +8,7 @@
 from jax.experimental.pallas import tpu as pltpu
 from jax.sharding import PartitionSpec as P
 
-SUB = 64
+SUB = 128
 PARTS = 8
 MASKED = -1e30
 MESH = pl.DeviceIdType.MESH

time: 22.3 us -> 22.6 us (1.013)
  Pallas kernels: 21.5 us -> 21.8 us
    pallas_call x1, Pallas kernels: 18.9 us -> 19.2 us  [shards(): pl.pallas_call(functools.partial(kernel, sizes), out_shape=shapes, in_spe...]
where the time goes in v7:
time: 22.6 us; the launch traced here: 22.5 us
  Pallas kernels  21.8 us (96%)
  between operations  0.64 us (3%)
    pallas_call x1, Pallas kernels, shards(): pl.pallas_call(functools.partial(kernel, sizes), out_shape=shapes, in_spe...  19.2 us
    pallas_call x1, Pallas kernels, shards(): pl.pallas_call(write, out_shape=shapes, in_specs=[hbm] * 3, out_specs=(hb...  2.6 us

profile of v7, /device:TPU:15, one launch (start us, length us, event | category | flops | bytes accessed | tf_op | source)
XLA Modules:
  0.0 22.5 jit_solution(1636134962651979900)
XLA Ops:
  0.6 19.2 %shard_map.85 = (bf16[128,64,128]{2,1,0:T(8,128)(2,1)}, bf16[128,8,128]{2,1,0:T(8,128)(2,1)}, bf16[128,8,128]{2,1,0:T(8,128)(2,1)}) custom-call(bf16[128,64,128]{2,1,0:T(8,128)(2,1)} %q_hbm.1, bf16[128,8,128]{2,1,0:T(8,128)(2,1)} %k_hbm.1, bf16[128,8,128]{2,1,0:T(8,128)(2,1)} %v_hbm.1, bf16[128,64,128]{2,1,0:T(8,128)(2,1)} %o_hbm.1, ...), custom_call_target="tpu_custom_call" | custom-call | flops 2684354560 | bytes 8388608 | tf_op jit(solution)/shard_map/pallas_call | solution.py:297
  19.9 2.6 %shard_map.86 = (bf16[128,64,128]{2,1,0:T(8,128)(2,1)}, bf16[128,8,128]{2,1,0:T(8,128)(2,1)}, bf16[128,8,128]{2,1,0:T(8,128)(2,1)}) custom-call(bf16[128,64,128]{2,1,0:T(8,128)(2,1)} %get-tuple-element.6.dq_in, bf16[128,8,128]{2,1,0:T(8,128)(2,1)} %get-tuple-element.7.dk_in, bf16[128,8,128]{2,1,0:T(8,128)(2,1)} %get-tuple-element.8.dv_in), custom_call_target="tpu_custom_call" | custom-call | tf_op jit(solution)/shard_map/pallas_call | solution.py:330
